TPU v7x, 256 devices: a whole 4x4x8 slice. The times are simulated.
256 devices in a mesh: space: 64 (over z, x, core), blk: 4 (over y).
Axes of the slice: x: 4, y: 4, z: 8, core: 2. Of those that a mesh axis runs over, the one named last changes fastest.
Arguments:
- start: float32 [262144, 128], P('space', 'blk')
- faces: int32 [4096, 6], P('space'), may hold values from -1 to 4095, as said below
- cavity: int32 [4096], P('space'), may hold values 0 or 1
- blocks: float32 [4096, 7, 64, 64], P('space'), as said below
Outputs:
- next_basis: float32 [262144, 128], P('space', 'blk')
- coefficients: float32 [5, 128, 128], P(None, None, 'blk')
Inputs may be any that keep to these rules, and one draw needn't show every extreme that they name: Elements are numbered layer by layer along the slab's third dimension, 64 to a layer, in an order within each layer that the draw sets; faces 0 to 5 look towards falling and rising first, second and third coordinates; an entry is -1 exactly where the face lies on the slab's outer boundary, else the element across the face, which lies in the same layer or the layers just below and above. Where faces[e, f] = n >= 0, blocks[e, f + 1] is the transpose of n's block for the opposite face; blocks[e, 0] is symmetric.
All inputs are finite; a program needn't handle non-finite values. No bound on the sum of `cavity` on one device may be relied on, other than what follows from the above.
Results may differ from a plain program's by a relative error of at most 0.0002.
Values sent between devices are 32-bit elements; how exact they have to be, the bound alone decides.
A program may use at most 128 MiB of HBM per device.

v0:
```python
import jax
import jax.numpy as jnp
from jax import lax
from jax.sharding import PartitionSpec as P

GX = 8
GY = 8


def padded_2(block, sides, width):
    for axis, dim in sides:
        count = lax.axis_size(axis)
        forward = [(i, i + 1) for i in range(count - 1)]
        backward = [(target, source) for source, target in forward]
        low = lax.ppermute(
            lax.slice_in_dim(block, block.shape[dim] - width, None, axis=dim), axis, forward
        )
        high = lax.ppermute(lax.slice_in_dim(block, 0, width, axis=dim), axis, backward)
        block = jnp.concatenate([low, block, high], axis=dim)
    return block


def gram_dot(left, right):
    return lax.dot_general(
        left,
        right,
        (((0,), (0,)), ((), ())),
        precision=lax.Precision.HIGHEST,
        preferred_element_type=jnp.float32,
    )


def times(left, right):
    return jnp.dot(left, right, precision=lax.Precision.HIGHEST, preferred_element_type=jnp.float32)


def factor_upper(gram_part):
    return jnp.linalg.cholesky(lax.psum(gram_part, "space")).T


def inverse_of(upper_factor):
    lower_inverse = jax.scipy.linalg.solve_triangular(
        upper_factor.T, jnp.eye(upper_factor.shape[0], dtype=jnp.float32), lower=True
    )
    return lower_inverse.T


def local(start, faces, cavity, blocks):
    elem_count = blocks.shape[0]
    dof_width = blocks.shape[-1]
    row_total = start.shape[0]
    narrow = start.shape[1]
    layer_size = GX * GY
    solid_mask = (1 - cavity).astype(jnp.float32)
    has_face = faces >= 0
    local_index = jnp.where(has_face, faces - lax.axis_index("space") * elem_count + layer_size, 0)
    face_weight = has_face.astype(jnp.float32)
    own_start = lax.axis_index("blk") * narrow
    face_blocks = blocks[:, 1:]

    def operate(vectors):
        masked = vectors.reshape(elem_count, dof_width, narrow) * solid_mask[:, None, None]
        inner_part = jnp.einsum(
            "epq,eqc->epc", blocks[:, 0], masked, precision=lax.Precision.HIGHEST
        )
        padded = padded_2(masked, (("space", 0),), layer_size)
        neighbours = jnp.take(padded, local_index, axis=0) * face_weight[:, :, None, None]
        outer_part = jnp.einsum(
            "efpq,efqc->epc", face_blocks, neighbours, precision=lax.Precision.HIGHEST
        )
        return ((inner_part + outer_part) * solid_mask[:, None, None]).reshape(row_total, narrow)

    def own_columns(matrix):
        return lax.dynamic_slice_in_dim(matrix, own_start, narrow, matrix.ndim - 1)

    def normalize(residue):
        gathered = lax.all_gather(residue, "blk", axis=1, tiled=True)
        upper_factor = factor_upper(gram_dot(gathered, gathered))
        return (times(gathered, inverse_of(upper_factor)), upper_factor)

    def project(basis_all, residue):
        return lax.psum(gram_dot(basis_all, residue), "space")

    basis_one, start_factor = normalize(start)
    residue = operate(own_columns(basis_one))
    alpha_one = project(basis_one, residue)
    residue = residue - times(basis_one, alpha_one)
    basis_two, beta_one = normalize(residue)
    beta_rows = lax.dynamic_slice_in_dim(beta_one, own_start, narrow, 0)
    residue = operate(own_columns(basis_two)) - times(basis_one, beta_rows.T)
    alpha_two = project(basis_two, residue)
    residue = residue - times(basis_two, alpha_two)
    basis_three, beta_two = normalize(residue)
    coefficients = jnp.stack(
        [
            own_columns(start_factor),
            alpha_one,
            own_columns(beta_one),
            alpha_two,
            own_columns(beta_two),
        ]
    )
    return (own_columns(basis_three), coefficients)


def solution(mesh):
    in_specs = (P("space", "blk"), P("space", None), P("space"), P("space", None, None, None))
    out_specs = (P("space", "blk"), P(None, None, "blk"))
    return jax.shard_map(local, mesh=mesh, in_specs=in_specs, out_specs=out_specs, check_vma=False)
```

profile of v0, /device:TPU:1, one launch (start us, length us, event | category | flops | bytes accessed | tf_op | source)
XLA Modules:
  0.0 1316.3 jit_solution(17743359390846614674)
XLA Ops:
  7.2 0.7 all-gather.4.cloned.1.call-update
  8.0 39.1 %all-gather.4.cloned.1.call-done = f32[4096,128]{0,1:T(8,128)} async-done(((f32[4096,32]{0,1:T(8,128)}), f32[4096,128]{0,1:T(8,128)}) %all-gather.4.cloned.1.call-update) | async-done | bytes 2097168 | tf_op jit(solution)/shard_map/all_gather | solution.py:77
  47.1 4.8 fusion.59
  52.0 168.1 %all-reduce.4.cloned.1.call-done = f32[128,128]{0,1:T(8,128)} async-done(((f32[128,128]{0,1:T(8,128)}), f32[128,128]{0,1:T(8,128)}) %all-reduce.4.cloned.1.call-update) | async-done | bytes 65552 | tf_op jit(solution)/shard_map/psum | solution.py:38
  220.1 0.9 copy.36
  221.0 0.9 fusion.51
  221.9 11.7 cholesky.59
  233.6 0.6 compare_reduce_fusion.2
  234.3 0.7 select_bitcast_fusion.2
  234.9 9.8 custom-call.7
  245.0 1.9 fusion.60
  246.9 1.4 copy-done
  248.4 0.4 reshape.31
  248.8 0.6 copy_multiply_fusion.1
  249.4 2.3 collective-permute-start.1
  251.7 3.7 collective-permute-start
  255.9 6.0 fusion.12
  262.0 3.6 collective-permute-done.1
  265.5 1.0 copy-done.10
  266.7 2.2 pad_maximum_fusion
  268.9 3.8 gather_fusion
  272.7 15.5 %fusion.37 = f32[64,64,32]{1,2,0:T(8,128)S(1)} fusion(f32[64,32,64]{2,1,0:T(8,128)} %fusion.12, f32[64,7,64,64]{3,2,1,0:T(8,128)} %param.12, f32[64,6,64,32]{2,3,1,0:T(8,128)} %bitcast.108, f32[64,6]{1,0:T(8,128)S(1)} %copy.41, pred[64,6]{1,0:T(8,128)(4,1)S(1)} %copy.39, f32[64]{0:T(128)S(1)} %subtract_convert_fusion), kind=kOutput, calls=%fused_computation.32 | convolution fusion | flops 605814784 | bytes 20449408 | tf_op jit(solution)/shard_map/efpq,efqc->epc/dot_general | solution.py:68
  288.3 1.6 copy.42
  289.8 1.6 reshape.32
  291.4 2.1 fusion.61
  293.5 241.0 %psum.36 = f32[128,32]{0,1:T(8,128)S(1)} all-reduce(f32[128,32]{0,1:T(8,128)S(1)} %fusion.61), channel_id=1, replica_groups=mesh['space'=64,'blk'=4] {'space'}, use_global_device_ids=true, to_apply=%region_3.7 | all-reduce | flops 4096 | bytes 32768 | tf_op jit(solution)/shard_map/psum | solution.py:82
  534.5 2.1 convolution_subtract_fusion.2
  536.8 41.0 %all-gather.6.cloned.1.call-done = f32[4096,128]{0,1:T(8,128)} async-done(((f32[4096,32]{0,1:T(8,128)}), f32[4096,128]{0,1:T(8,128)}) %all-gather.6.cloned.1.call-update) | async-done | bytes 2097168 | tf_op jit(solution)/shard_map/all_gather | solution.py:77
  577.8 4.8 fusion.62
  582.7 168.1 %all-reduce.6.cloned.1.call-done = f32[128,128]{0,1:T(8,128)} async-done(((f32[128,128]{0,1:T(8,128)}), f32[128,128]{0,1:T(8,128)}) %all-reduce.6.cloned.1.call-update) | async-done | bytes 65552 | tf_op jit(solution)/shard_map/psum | solution.py:38
  750.8 0.9 copy.44
  751.7 0.9 fusion.49
  752.6 11.7 cholesky.70
  764.3 0.6 compare_reduce_fusion.1
  765.0 0.7 select_bitcast_fusion.1
  765.7 9.8 custom-call.8
  775.8 2.0 fusion.63
  777.8 1.3 copy-done.3
  779.6 0.6 copy_multiply_fusion
  780.2 2.3 collective-permute-start.3
  782.5 3.7 collective-permute-start.2
  786.2 6.0 fusion.10
  792.1 4.2 collective-permute-done.3
  796.3 1.2 collective-permute-done.2
  797.9 3.8 gather_fusion.1
  801.7 15.5 %fusion.28 = f32[64,64,32]{1,2,0:T(8,128)S(1)} fusion(f32[64,32,64]{2,1,0:T(8,128)} %fusion.10, f32[64,7,64,64]{3,2,1,0:T(8,128)} %param.12, f32[64,6,64,32]{2,3,1,0:T(8,128)} %bitcast.107, f32[64,6]{1,0:T(8,128)S(1)} %copy.41, pred[64,6]{1,0:T(8,128)(4,1)S(1)} %copy.39, f32[64]{0:T(128)S(1)} %subtract_convert_fusion), kind=kOutput, calls=%fused_computation.29 | convolution fusion | flops 605814784 | bytes 20449408 | tf_op jit(solution)/shard_map/efpq,efqc->epc/dot_general | solution.py:68
  817.2 0.6 copy.48
  817.8 1.2 reshape.34
  819.0 2.5 convolution_subtract_fusion.1
  821.5 2.1 fusion.64
  823.6 241.0 %psum.38 = f32[128,32]{0,1:T(8,128)S(1)} all-reduce(f32[128,32]{0,1:T(8,128)S(1)} %fusion.64), channel_id=1, replica_groups=mesh['space'=64,'blk'=4] {'space'}, use_global_device_ids=true, to_apply=%region_5.9 | all-reduce | flops 4096 | bytes 32768 | tf_op jit(solution)/shard_map/psum | solution.py:82
  1064.5 2.1 convolution_subtract_fusion
  1066.9 40.9 %all-gather.8.cloned.1.call-done = f32[4096,128]{0,1:T(8,128)} async-done(((f32[4096,32]{0,1:T(8,128)}), f32[4096,128]{0,1:T(8,128)}) %all-gather.8.cloned.1.call-update) | async-done | bytes 2097168 | tf_op jit(solution)/shard_map/all_gather | solution.py:77
  1107.8 4.8 fusion.65
  1112.6 168.1 %all-reduce.8.cloned.1.call-done = f32[128,128]{0,1:T(8,128)} async-done(((f32[128,128]{0,1:T(8,128)}), f32[128,128]{0,1:T(8,128)}) %all-reduce.8.cloned.1.call-update) | async-done | bytes 65552 | tf_op jit(solution)/shard_map/psum | solution.py:38
  1280.8 0.9 copy.50
  1281.7 0.9 fusion.47
  1282.6 11.7 cholesky.81
  1294.3 0.6 compare_reduce_fusion
  1295.0 0.7 select_bitcast_fusion
  1295.6 9.8 custom-call.9
  1305.7 2.0 fusion.66
  1307.8 0.8 constant_dynamic-slice_fusion
  1308.6 0.6 copy-done.12
  (58 shorter events, 3.2 us)
Async XLA Ops:
  7.2 39.9 %all-gather.4.cloned.1.call-start = ((), (), s32[]{:S(2)}) async-start(), calls=%async_computation | async-start | bytes 2621440 | tf_op jit(solution)/shard_map/all_gather | solution.py:77
  7.9 44.1 %copy-start.13 = (s32[64]{0:T(128)S(1)}, s32[64]{0:T(128)}, u32[]{:S(2)}) copy-start(s32[64]{0:T(128)} %param.11) | copy-start | bytes 772
  7.9 212.2 %all-reduce.4.cloned.1.call-start = ((), (), s32[]{:S(2)}) async-start(), calls=%async_computation.1 | async-start | bytes 131072 | tf_op jit(solution)/shard_map/psum | solution.py:38
  47.1 198.0 %copy-start.6 = (f32[4096,128]{0,1:T(8,128)S(1)}, f32[4096,128]{0,1:T(8,128)}, u32[]{:S(2)}) copy-start(f32[4096,128]{0,1:T(8,128)} %all-gather.4.cloned.1.call-done) | copy-start | bytes 6291460
  51.9 525.9 %all-gather.6.cloned.1.call-start = ((), (), s32[]{:S(2)}) async-start(), calls=%async_computation.2 | async-start | bytes 2621440 | tf_op jit(solution)/shard_map/all_gather | solution.py:77
  246.9 1.4 copy-start
  248.3 7.1 copy-start.11
  249.4 12.6 copy-start.9
  249.4 16.1 %collective-permute-start.1 = (f32[64,64,32]{1,2,0:T(8,128)S(1)}, f32[64,64,32]{1,2,0:T(8,128)S(1)}, u32[]{:S(2)}, u32[]{:S(2)}) collective-permute-start(f32[64,64,32]{1,2,0:T(8,128)S(1)} %copy_multiply_fusion.1), channel_id=1, source_target_pairs={{4,0},{8,4},{12,8},{16,12},{20,16},{24,20},{28,24},{32,28},{36,32}... | collective-permute-start | bytes 1572872 | tf_op jit(solution)/shard_map/ppermute | solution.py:18
  251.7 15.0 %collective-permute-start = (f32[64,64,32]{1,2,0:T(8,128)S(1)}, f32[64,64,32]{1,2,0:T(8,128)}, u32[]{:S(2)}, u32[]{:S(2)}) collective-permute-start(f32[64,64,32]{1,2,0:T(8,128)S(1)} %copy_multiply_fusion.1), channel_id=1, source_target_pairs={{0,4},{4,8},{8,12},{12,16},{16,20},{20,24},{24,28},{28,32},{32,36}... | collective-permute-start | bytes 1572872 | tf_op jit(solution)/shard_map/ppermute | solution.py:15
  265.5 1.0 copy-start.10
  288.3 3.2 copy-start.1
  536.5 214.3 %all-reduce.6.cloned.1.call-start = ((), (), s32[]{:S(2)}) async-start(), calls=%async_computation.3 | async-start | bytes 131072 | tf_op jit(solution)/shard_map/psum | solution.py:38
  577.8 198.0 %copy-start.8 = (f32[4096,128]{0,1:T(8,128)S(1)}, f32[4096,128]{0,1:T(8,128)}, u32[]{:S(2)}) copy-start(f32[4096,128]{0,1:T(8,128)} %all-gather.6.cloned.1.call-done) | copy-start | bytes 6291460
  582.7 525.1 %all-gather.8.cloned.1.call-start = ((), (), s32[]{:S(2)}) async-start(), calls=%async_computation.4 | async-start | bytes 2621440 | tf_op jit(solution)/shard_map/all_gather | solution.py:77
  777.8 1.4 copy-start.3
  780.2 16.1 %collective-permute-start.3 = (f32[64,64,32]{1,2,0:T(8,128)S(1)}, f32[64,64,32]{1,2,0:T(8,128)S(1)}, u32[]{:S(2)}, u32[]{:S(2)}) collective-permute-start(f32[64,64,32]{1,2,0:T(8,128)S(1)} %copy_multiply_fusion), channel_id=1, source_target_pairs={{4,0},{8,4},{12,8},{16,12},{20,16},{24,20},{28,24},{32,28},{36,32}... | collective-permute-start | bytes 1572872 | tf_op jit(solution)/shard_map/ppermute | solution.py:18
  782.5 15.0 %collective-permute-start.2 = (f32[64,64,32]{1,2,0:T(8,128)S(1)}, f32[64,64,32]{1,2,0:T(8,128)S(1)}, u32[]{:S(2)}, u32[]{:S(2)}) collective-permute-start(f32[64,64,32]{1,2,0:T(8,128)S(1)} %copy_multiply_fusion), channel_id=1, source_target_pairs={{0,4},{4,8},{8,12},{12,16},{16,20},{20,24},{24,28},{28,32},{32,36}... | collective-permute-start | bytes 1572872 | tf_op jit(solution)/shard_map/ppermute | solution.py:15
  817.2 1.8 copy-start.2
  819.0 2.5 copy-start.4
  821.5 243.0 %copy-start.5 = (f32[4096,128]{0,1:T(8,128)S(1)}, f32[4096,128]{0,1:T(8,128)}, u32[]{:S(2)}) copy-start(f32[4096,128]{0,1:T(8,128)} %copy-done.3) | copy-start | bytes 6291460
  1066.6 214.2 %all-reduce.8.cloned.1.call-start = ((), (), s32[]{:S(2)}) async-start(), calls=%async_computation.5 | async-start | bytes 131072 | tf_op jit(solution)/shard_map/psum | solution.py:38
  1107.8 198.0 %copy-start.7 = (f32[4096,128]{0,1:T(8,128)S(1)}, f32[4096,128]{0,1:T(8,128)}, u32[]{:S(2)}) copy-start(f32[4096,128]{0,1:T(8,128)} %all-gather.8.cloned.1.call-done) | copy-start | bytes 6291460
  1308.6 0.6 copy-start.12
Sparse Core Ops, SparseCore 0:
  9.8 37.2 all-gather.3
  52.0 167.9 all-reduce.3
  536.7 41.0 all-gather.5
  582.8 167.9 all-reduce.5
  1066.7 40.9 all-gather.7
  1112.8 167.9 all-reduce.7
where the time goes:
time: 1330 us; the launch traced here: 1320 us
  waiting for transfers between devices  635 us (48%)
  blocking collectives  482 us (36%)
  other arithmetic  75 us (6%)
  matrix products  74.9 us (6%)
  local copies, waits for them, and re-layouts  21.9 us (2%)
  between operations  14.7 us (1%)
    psum x3, waiting for transfers between devices, factor_upper(): return jnp.linalg.cholesky(lax.psum(gram_part, 'space')).T  504 us
    psum x2, blocking collectives, project(): return lax.psum(gram_dot(basis_all, residue), 'space')  482 us
    all_gather x3, waiting for transfers between devices, normalize(): gathered = lax.all_gather(residue, 'blk', axis=1, tiled=True)  121 us
    another operation x9, other arithmetic, factor_upper(): return jnp.linalg.cholesky(lax.psum(gram_part, 'space')).T  37.2 us
    another operation x6, other arithmetic, inverse_of(): jax.scipy.linalg.solve_triangular(upper_factor.T, jnp.eye(upper_factor.sh...  31.4 us
    dot_general x2, matrix products, operate(): jnp.einsum('efpq,efqc->epc', face_blocks, neighbours, precision=lax.Preci...  31 us
  transfers between devices with their start and end apart: 10, of which 10 were waited for; matrix products, arithmetic and copies ran while one was open for 1% of the time, Pallas kernels for 0%

commit v1 on v0

v1 whole, which is shorter than its diff:
```python
import jax
import jax.numpy as jnp
from jax import lax
from jax.experimental import pallas as pl
from jax.experimental.pallas import tpu as pltpu
from jax.sharding import PartitionSpec as P

LAYER = 64
DOF = 64
ROWS = LAYER * DOF
K = 128
CORES = 2
XS = 4
ZS = 8
YS = 4
SPACE = ZS * XS * CORES
NARROW = K // YS
SIDES = 7
NONE = 3 * LAYER
WIDE = 32
SUB = 8
CHUNK = 512
STAGED = 16
MESH = pl.DeviceIdType.MESH
F32 = jnp.float32
BF16 = jnp.bfloat16


def dot(left, right, left_dim, right_dim):
    return lax.dot_general(
        left,
        right,
        (((left_dim,), (right_dim,)), ((), ())),
        precision=lax.Precision.HIGHEST,
        preferred_element_type=F32,
    )


def times(left, right):
    return dot(left, right, 1, 0)


def cross(left, right):
    return dot(left, right, 1, 1)


def split(value):
    first = value.astype(BF16)
    rest = value - first.astype(F32)
    second = rest.astype(BF16)
    return first, second, (rest - second.astype(F32)).astype(BF16)


def eliminate(gram, unit, first):
    shape = gram.shape
    row_id = lax.broadcasted_iota(jnp.int32, shape, 0)
    for sub in range(0, WIDE, SUB):
        columns = [
            jnp.broadcast_to(gram[:, first + sub + j : first + sub + j + 1], shape)
            for j in range(SUB)
        ]
        for j in range(SUB):
            k = sub + j
            scale = lax.rsqrt(jnp.broadcast_to(columns[j][k : k + 1], shape))
            pivot_gram = jnp.broadcast_to(gram[k : k + 1], shape) * scale
            pivot_unit = jnp.broadcast_to(unit[k : k + 1], shape) * scale
            factor = columns[j] * scale
            below = jnp.where(row_id > k, factor, 0.0)
            for other in range(j + 1, SUB):
                near = jnp.broadcast_to(factor[sub + other : sub + other + 1], shape)
                columns[other] = columns[other] - below * near
            gram = jnp.where(row_id == k, pivot_gram, gram - below * pivot_gram)
            unit = jnp.where(row_id == k, pivot_unit, unit - below * pivot_unit)
    return gram, unit


def factor_gram(gram_ref, upper, inverse):
    row_id = lax.broadcasted_iota(jnp.int32, (WIDE, K), 0)
    col_id = lax.broadcasted_iota(jnp.int32, (WIDE, K), 1)
    for first in range(0, K, WIDE):
        rows = pl.ds(first, WIDE)
        gram = gram_ref[rows, :]
        unit = jnp.where(row_id + first == col_id, 1.0, 0.0)
        if first:
            above_gram = upper[pl.ds(0, first), :]
            above_unit = inverse[pl.ds(0, first), :]
            left = above_gram[:, first : first + WIDE]
            gram = gram - dot(left, above_gram, 0, 0)
            unit = unit - dot(left, above_unit, 0, 0)
        gram, unit = eliminate(gram, unit, first)
        upper[rows, :] = jnp.where(row_id + first <= col_id, gram, 0.0)
        inverse[rows, :] = unit


def prepare(staged, packed, base):
    def body(elem, carry):
        for pair in range(4):
            if pair < 3:
                right = staged[elem, 2 * pair + 1]
            else:
                right = jnp.zeros((DOF, DOF), F32)
            both = jnp.concatenate([staged[elem, 2 * pair], right], axis=1)
            for piece, value in enumerate(split(both)):
                packed[base + elem, piece, :, pair * 128 : (pair + 1) * 128] = value
        return carry

    lax.fori_loop(0, STAGED, body, 0, unroll=2)


def spread(source, elems, base):
    is_low = lax.broadcasted_iota(jnp.int32, (NARROW, 2 * DOF), 1) < DOF

    def body(pair, carry):
        straight = source[:, pl.ds(pl.multiple_of(pair * 128, 128), 128)]
        turned = pltpu.roll(straight, DOF, 1)
        for side, low, high in ((0, straight, turned), (1, turned, straight)):
            place = base + 2 * pair + side
            for piece, value in enumerate(split(jnp.where(is_low, low, 0.0))):
                elems[0, place, piece] = value
            for piece, value in enumerate(split(jnp.where(is_low, 0.0, high))):
                elems[1, place, piece] = value
        return carry

    lax.fori_loop(0, LAYER // 2, body, 0, unroll=2)


def operate(index, elems, packed, mask, out, own_rows):
    def product(left, right):
        return lax.dot_general(
            left, right, (((1,), (1,)), ((), ())), preferred_element_type=F32
        )

    def one(elem):
        at = [index[elem * SIDES + side] for side in range(SIDES)]
        pieces = []
        for piece in range(3):
            pairs = [
                elems[0, at[2 * pair], piece] + elems[1, at[2 * pair + 1], piece]
                for pair in range(3)
            ]
            pairs.append(elems[0, at[6], piece])
            pieces.append(jnp.concatenate(pairs, axis=1))
        three = product(jnp.concatenate(pieces, axis=0), packed[elem, 0])
        two = product(jnp.concatenate(pieces[:2], axis=0), packed[elem, 1])
        last = product(pieces[0], packed[elem, 2])
        small = three[2 * NARROW :] + two[NARROW:] + last
        return three[:NARROW] + (three[NARROW : 2 * NARROW] + two[:NARROW] + small)

    def body(pair, carry):
        both = jnp.concatenate([one(2 * pair), one(2 * pair + 1)], axis=1)
        cols = pl.ds(pl.multiple_of(pair * 128, 128), 128)
        out[own_rows, cols] = both * mask[:, cols]
        return carry

    lax.fori_loop(0, LAYER // 2, body, 0, unroll=4)


def kernel(
    index,
    start,
    mask,
    blocks,
    basis_out,
    coef_out,
    basis,
    image,
    second,
    send_0,
    low_0,
    high_0,
    send_1,
    low_1,
    high_1,
    elems,
    packed,
    staged,
    near_0,
    far_0,
    done_0,
    near_1,
    far_1,
    done_1,
    near_2,
    far_2,
    done_2,
    part_0,
    part_1,
    part_2,
    gram,
    upper,
    inverse,
    alpha,
    flip,
    stage_sem,
    halo_send,
    halo_recv,
    rows_send,
    rows_recv,
    sums_send,
    sums_recv,
):
    space = lax.axis_index("space")
    blk = lax.axis_index("blk")
    core = lax.rem(space, CORES)
    spot = lax.rem(space, XS * CORES)
    plane = space // (XS * CORES)
    plane_base = plane * (XS * CORES)
    quad = blk * CORES + core
    own_rows = pl.ds(pl.multiple_of(blk * NARROW, NARROW), NARROW)
    above = (lax.rem(space + 1, SPACE), blk)
    below = (lax.rem(space + SPACE - 1, SPACE), blk)
    near_ids = [lax.rem(spot + step, 8) for step in range(1, 8)]
    near_devices = [(plane_base + near, blk) for near in near_ids]
    far_devices = [(lax.rem(plane + step, 8) * 8 + spot, blk) for step in range(1, 8)]
    quads = [lax.rem(quad + step, 8) for step in range(1, 8)]
    done_devices = [(space - core + lax.rem(q, CORES), q // CORES) for q in quads]

    def stage_copy(part):
        return pltpu.make_async_copy(
            blocks.at[pl.ds(part * STAGED, STAGED)], staged.at[part % 2], stage_sem.at[part % 2]
        )

    stage_copy(0).start()
    stage_copy(1).start()
    barrier = pltpu.get_barrier_semaphore()
    for device in near_devices + far_devices + done_devices + [above, below]:
        pl.semaphore_signal(barrier, inc=1, device_id=device, device_id_type=MESH)
    basis[own_rows, :] = start[...]
    send_0[...] = start[...] * mask[...]
    pl.semaphore_wait(barrier, 23)

    def halo(call, source, low, high):
        copies = [
            pltpu.make_async_remote_copy(
                src_ref=source,
                dst_ref=target,
                send_sem=halo_send.at[call, way],
                recv_sem=halo_recv.at[call, way],
                device_id=device,
                device_id_type=MESH,
            )
            for way, target, device in ((0, low, above), (1, high, below))
        ]
        for copy in copies:
            copy.start()
        return copies

    def gather(call, array):
        copies = []
        for step in range(1, YS):
            copy = pltpu.make_async_remote_copy(
                src_ref=array.at[own_rows],
                dst_ref=array.at[own_rows],
                send_sem=rows_send.at[call, step - 1],
                recv_sem=rows_recv.at[call, step - 1],
                device_id=(space, lax.rem(blk + step, YS)),
                device_id_type=MESH,
            )
            copy.start()
            copies.append(copy)
        return copies

    def wait(copies):
        for copy in copies:
            copy.wait()

    def exchange(call, stage, sources, slots, mine, devices):
        copies = []
        for step in range(7):
            copy = pltpu.make_async_remote_copy(
                src_ref=sources[step],
                dst_ref=slots.at[mine],
                send_sem=sums_send.at[call, stage, step],
                recv_sem=sums_recv.at[call, stage, step],
                device_id=devices[step],
                device_id_type=MESH,
            )
            copy.start()
            copies.append(copy)
        return copies

    def total(slots):
        value = slots[0]
        for slot in range(1, 8):
            value = value + slots[slot]
        return value

    def reduce_all(call, part, near, far, done):
        half = part.shape[0] // CORES
        sources = [
            part.at[pl.ds(pl.multiple_of(lax.rem(spot_id, CORES) * half, 8), half)]
            for spot_id in near_ids
        ]
        copies = exchange(call, 0, sources, near, spot, near_devices)
        near[spot] = part[pl.ds(pl.multiple_of(core * half, 8), half), :]
        wait(copies)
        far[plane] = total(near)
        wait(exchange(call, 1, [far.at[plane]] * 7, far, plane, far_devices))
        done[quad] = total(far)
        wait(exchange(call, 2, [done.at[quad]] * 7, done, quad, done_devices))

    def square(done, which):
        rows = []
        for member in range(YS):
            panel = jnp.concatenate([done[2 * member], done[2 * member + 1]], axis=0)
            rows.append(panel[which * NARROW : (which + 1) * NARROW])
        return jnp.concatenate(rows, axis=0)

    def over_chunks(body, init):
        def step(chunk, carry):
            return body(pl.ds(pl.multiple_of(chunk * CHUNK, CHUNK), CHUNK), carry)

        return lax.fori_loop(0, ROWS // CHUNK, step, init)

    def keep_upper(which):
        flip[...] = upper[...].T
        coef_out[which] = flip[own_rows, :]

    halo_copies = halo(0, send_0, low_0, high_0)
    start_copies = gather(0, basis)
    for part in range(LAYER // STAGED):
        stage_copy(part).wait()
        prepare(staged.at[part % 2], packed, part * STAGED)
        if part + 2 < LAYER // STAGED:
            stage_copy(part + 2).start()
    for which in range(2):
        for piece in range(3):
            elems[which, NONE, piece] = jnp.zeros((NARROW, 2 * DOF), BF16)
    spread(send_0, elems, LAYER)
    wait(halo_copies)
    spread(low_0, elems, 0)
    spread(high_0, elems, 2 * LAYER)
    operate(index, elems, packed, mask, image, own_rows)
    image_copies = gather(1, image)
    wait(start_copies)

    def start_products(cols, carry):
        left = jnp.concatenate([basis[own_rows, cols], image[own_rows, cols]], axis=0)
        return carry + cross(left, basis[:, cols])

    part_0[...] = over_chunks(start_products, jnp.zeros(part_0.shape, F32))
    reduce_all(0, part_0, near_0, far_0, done_0)
    gram[...] = square(done_0, 0)
    factor_gram(gram, upper, inverse)
    alpha[...] = cross(times(inverse[...], square(done_0, 1)), inverse[...])
    coef_out[1] = alpha[own_rows, :]
    keep_upper(0)
    wait(image_copies)

    def first_residue(cols, carry):
        vectors = times(inverse[...], basis[:, cols])
        basis[:, cols] = vectors
        image[:, cols] = times(inverse[...], image[:, cols]) - times(alpha[...], vectors)
        return carry

    over_chunks(first_residue, 0)

    send_1[...] = image[own_rows, :] * mask[...]
    halo_copies = halo(1, send_1, low_1, high_1)
    spread(send_1, elems, LAYER)
    wait(halo_copies)
    spread(low_1, elems, 0)
    spread(high_1, elems, 2 * LAYER)
    operate(index, elems, packed, mask, second, own_rows)
    second_copies = gather(2, second)

    def residue_products(cols, carry):
        left = jnp.concatenate([image[own_rows, cols], second[own_rows, cols]], axis=0)
        return (
            carry[0] + cross(left, image[:, cols]),
            carry[1] + cross(image[own_rows, cols], basis[:, cols]),
        )

    products = over_chunks(
        residue_products, (jnp.zeros((2 * NARROW, K), F32), jnp.zeros((NARROW, K), F32))
    )
    part_1[pl.ds(0, 2 * NARROW), :] = products[0]
    part_1[pl.ds(2 * NARROW, NARROW), :] = products[1]
    reduce_all(1, part_1, near_1, far_1, done_1)
    gram[...] = square(done_1, 0)
    factor_gram(gram, upper, inverse)
    skew = times(inverse[...], square(done_1, 2))
    inner = cross(times(inverse[...], square(done_1, 1)), inverse[...])
    alpha[...] = inner - cross(upper[...], skew)
    coef_out[3] = alpha[own_rows, :]
    keep_upper(2)
    wait(second_copies)

    def second_residue(cols, carry):
        vectors = times(inverse[...], image[:, cols])
        value = times(inverse[...], second[:, cols]) - times(upper[...], basis[:, cols])
        second[:, cols] = value - times(alpha[...], vectors)
        return carry

    over_chunks(second_residue, 0)

    def last_products(cols, carry):
        return carry + cross(second[own_rows, cols], second[:, cols])

    part_2[...] = over_chunks(last_products, jnp.zeros(part_2.shape, F32))
    reduce_all(2, part_2, near_2, far_2, done_2)
    gram[...] = square(done_2, 0)
    factor_gram(gram, upper, inverse)
    keep_upper(4)

    def last_basis(cols, carry):
        basis_out[:, cols] = times(inverse[own_rows, :], second[:, cols])
        return carry

    over_chunks(last_basis, 0)


def local(start, faces, cavity, blocks):
    elem_count = blocks.shape[0]
    shift = LAYER - lax.axis_index("space") * elem_count
    beside = jnp.where(faces >= 0, faces + shift, NONE)
    here = LAYER + jnp.arange(elem_count, dtype=jnp.int32)
    index = jnp.concatenate([here[:, None], beside], axis=1).reshape(-1)
    mask = jnp.repeat((1 - cavity).astype(F32), DOF)[None, :]
    vmem = pl.BlockSpec(memory_space=pltpu.VMEM)

    def slots(rows):
        return [pltpu.VMEM((8, rows // CORES, K), F32)] * 3

    basis, coefficients = pl.pallas_call(
        kernel,
        out_shape=(
            jax.ShapeDtypeStruct((NARROW, ROWS), F32),
            jax.ShapeDtypeStruct((5, NARROW, K), F32),
        ),
        in_specs=[
            pl.BlockSpec(memory_space=pltpu.SMEM),
            vmem,
            vmem,
            pl.BlockSpec(memory_space=pl.ANY),
        ],
        out_specs=(vmem, vmem),
        scratch_shapes=[pltpu.VMEM((K, ROWS), F32)] * 3
        + [pltpu.VMEM((NARROW, ROWS), F32)] * 6
        + [
            pltpu.VMEM((2, NONE + 1, 3, NARROW, 2 * DOF), BF16),
            pltpu.VMEM((LAYER, 3, DOF, 8 * DOF), BF16),
            pltpu.VMEM((2, STAGED, SIDES, DOF, DOF), F32),
        ]
        + slots(2 * NARROW)
        + slots(3 * NARROW)
        + slots(NARROW)
        + [pltpu.VMEM((count * NARROW, K), F32) for count in (2, 3, 1)]
        + [pltpu.VMEM((K, K), F32)] * 5
        + [
            pltpu.SemaphoreType.DMA((2,)),
            pltpu.SemaphoreType.DMA((2, 2)),
            pltpu.SemaphoreType.DMA((2, 2)),
            pltpu.SemaphoreType.DMA((3, YS - 1)),
            pltpu.SemaphoreType.DMA((3, YS - 1)),
            pltpu.SemaphoreType.DMA((3, 3, 7)),
            pltpu.SemaphoreType.DMA((3, 3, 7)),
        ],
        compiler_params=pltpu.CompilerParams(
            collective_id=1, has_side_effects=True, vmem_limit_bytes=60 * 2**20
        ),
    )(index, start.T, mask, blocks)
    return basis.T, jnp.swapaxes(coefficients, 1, 2)


def solution(mesh):
    in_specs = (P("space", "blk"), P("space", None), P("space"), P("space", None, None, None))
    out_specs = (P("space", "blk"), P(None, None, "blk"))
    return jax.shard_map(local, mesh=mesh, in_specs=in_specs, out_specs=out_specs, check_vma=False)
```

time: 1330 us -> 158 us (0.12); the launches traced: 1320 us -> 158 us
  waiting for transfers between devices: 635 us -> 0 us
  blocking collectives: 482 us -> 0 us
  Pallas kernels: 0 us -> 151 us
  matrix products: 74.9 us -> 0 us
  other arithmetic: 75 us -> 1.36 us
  local copies, waits for them, and re-layouts: 21.9 us -> 4.98 us
  between operations: 14.7 us -> 0.65 us
    psum x3 -> x0, waiting for transfers between devices: 504 us -> none  [factor_upper(): return jnp.linalg.cholesky(lax.psum(gram_part, 'space')).T]
    psum x2 -> x0, blocking collectives: 482 us -> none  [project(): return lax.psum(gram_dot(basis_all, residue), 'space')]
    pallas_call x0 -> x1, Pallas kernels: none -> 151 us  [local(): pl.pallas_call(kernel, out_shape=(jax.ShapeDtypeStruct((NARROW, ROWS), F3...]
    all_gather x3 -> x0, waiting for transfers between devices: 121 us -> none  [normalize(): gathered = lax.all_gather(residue, 'blk', axis=1, tiled=True)]
    dot_general x15 -> x0, matrix products: 74.1 us -> none  [the longest x2 31 us: operate(): jnp.einsum('efpq,efqc->epc', face_blocks, neighbours, precision=lax.Preci...]
    another operation x15 -> x0, other arithmetic: 68.6 us -> none  [the longest x9 37.2 us: factor_upper(): return jnp.linalg.cholesky(lax.psum(gram_part, 'space')).T]
  transfers between devices with their start and end apart: 10 -> 0, of which waited for: 10 -> 0; matrix products, arithmetic and copies ran while one was open for 1% -> 0% of each run, Pallas kernels for 0% -> 0%
where the time goes in v1:
time: 158 us
  Pallas kernels  151 us (96%)
  local copies, waits for them, and re-layouts  4.98 us (3%)
    pallas_call x1, Pallas kernels, local(): pl.pallas_call(kernel, out_shape=(jax.ShapeDtypeStruct((NARROW, ROWS), F3...  151 us
    unnamed x2, local copies, waits for them, and re-layouts  3.4 us

profile of v1, /device:TPU:1, one launch (start us, length us, event | category | flops | bytes accessed | tf_op | source)
XLA Modules:
  0.0 157.8 jit_solution(9597809180148393505)
XLA Ops:
  0.6 0.7 subtract_convert_fusion
  1.3 0.7 add_select_fusion
  2.0 0.1 copy.6
  2.1 0.7 reshape.14.index
  2.8 0.1 broadcast_in_dim.9
  2.9 0.7 broadcast_in_dim_reshape.3.mask
  3.6 150.8 %shard_map.59 = (f32[32,4096]{1,0:T(8,128)}, f32[5,32,128]{2,1,0:T(8,128)}) custom-call(s32[448]{0:T(512)} %reshape.14.index, f32[32,4096]{1,0:T(8,128)} %bitcast.3, f32[1,4096]{1,0:T(1,128)} %broadcast_in_dim_reshape.3.mask, f32[64,7,64,64]{3,2,1,0:T(8,128)} %blocks.1), custom_call_target="tpu_custom_call" | custom-call | tf_op jit(solution)/shard_map/pallas_call | solution.py:425
  154.4 1.9 %copy.9 = f32[4096,32]{0,1:T(8,128)} copy(f32[4096,32]{0,1:T(8,128)} %bitcast.4) | data formatting | bytes 1048576
  156.3 1.5 copy.10
  (2 shorter events, 0.0 us)

commit v2 on v1

v2 whole, which is shorter than its diff:
```python
import jax
import jax.numpy as jnp
from jax import lax
from jax.experimental import pallas as pl
from jax.experimental.pallas import tpu as pltpu
from jax.sharding import PartitionSpec as P

LAYER = 64
DOF = 64
ROWS = LAYER * DOF
K = 128
CORES = 2
XS = 4
ZS = 8
YS = 4
SPACE = ZS * XS * CORES
NARROW = K // YS
SIDES = 7
PARTS = 4
PART = ROWS // PARTS
HALF = ROWS // 2
NONE = 3 * LAYER
WIDE = 32
SUB = 8
CHUNK = 512
STAGED = 16
MESH = pl.DeviceIdType.MESH
F32 = jnp.float32
BF16 = jnp.bfloat16


def dot(left, right, left_dim, right_dim):
    return lax.dot_general(
        left,
        right,
        (((left_dim,), (right_dim,)), ((), ())),
        precision=lax.Precision.HIGHEST,
        preferred_element_type=F32,
    )


def times(left, right):
    return dot(left, right, 1, 0)


def cross(left, right):
    return dot(left, right, 1, 1)


def split(value):
    first = value.astype(BF16)
    rest = value - first.astype(F32)
    second = rest.astype(BF16)
    return first, second, (rest - second.astype(F32)).astype(BF16)


def eliminate(gram, unit, first):
    shape = gram.shape
    row_id = lax.broadcasted_iota(jnp.int32, shape, 0)
    for sub in range(0, WIDE, SUB):
        columns = [
            jnp.broadcast_to(gram[:, first + sub + j : first + sub + j + 1], shape)
            for j in range(SUB)
        ]
        for j in range(SUB):
            k = sub + j
            scale = lax.rsqrt(jnp.broadcast_to(columns[j][k : k + 1], shape))
            pivot_gram = jnp.broadcast_to(gram[k : k + 1], shape) * scale
            pivot_unit = jnp.broadcast_to(unit[k : k + 1], shape) * scale
            below = jnp.where(row_id > k, columns[j], 0.0) * scale
            for other in range(j + 1, SUB):
                near = jnp.broadcast_to(columns[j][sub + other : sub + other + 1], shape)
                columns[other] = columns[other] - below * (near * scale)
            gram = jnp.where(row_id == k, pivot_gram, gram - below * pivot_gram)
            unit = jnp.where(row_id == k, pivot_unit, unit - below * pivot_unit)
    return gram, unit


def factor_rows(gram_ref, upper, inverse, first):
    row_id = lax.broadcasted_iota(jnp.int32, (WIDE, K), 0)
    col_id = lax.broadcasted_iota(jnp.int32, (WIDE, K), 1)
    rows = pl.ds(first, WIDE)
    gram = gram_ref[rows, :]
    unit = jnp.where(row_id + first == col_id, 1.0, 0.0)
    if first:
        above_gram = upper[pl.ds(0, first), :]
        above_unit = inverse[pl.ds(0, first), :]
        left = above_gram[:, first : first + WIDE]
        gram = gram - dot(left, above_gram, 0, 0)
        unit = unit - dot(left, above_unit, 0, 0)
    gram, unit = eliminate(gram, unit, first)
    upper[rows, :] = jnp.where(row_id + first <= col_id, gram, 0.0)
    inverse[rows, :] = unit


def factor_gram(gram_ref, upper, inverse):
    for first in range(0, K, WIDE):
        factor_rows(gram_ref, upper, inverse, first)


def prepare(staged, packed, base):
    def body(elem, carry):
        for pair in range(4):
            if pair < 3:
                right = staged[elem, 2 * pair + 1]
            else:
                right = jnp.zeros((DOF, DOF), F32)
            both = jnp.concatenate([staged[elem, 2 * pair], right], axis=1)
            for piece, value in enumerate(split(both)):
                packed[base + elem, piece, :, pair * 128 : (pair + 1) * 128] = value
        return carry

    lax.fori_loop(0, STAGED, body, 0, unroll=2)


def spread(source, elems, base, part):
    is_low = lax.broadcasted_iota(jnp.int32, (NARROW, 2 * DOF), 1) < DOF

    count = LAYER // 2 // PARTS

    def body(step, carry):
        pair = part * count + step
        straight = source[:, pl.ds(pl.multiple_of(pair * 128, 128), 128)]
        turned = pltpu.roll(straight, DOF, 1)
        for side, low, high in ((0, straight, turned), (1, turned, straight)):
            place = base + 2 * pair + side
            for piece, value in enumerate(split(jnp.where(is_low, low, 0.0))):
                elems[0, place, piece] = value
            for piece, value in enumerate(split(jnp.where(is_low, 0.0, high))):
                elems[1, place, piece] = value
        return carry

    lax.fori_loop(0, count, body, 0, unroll=2)


def solid(cavity, elem):
    return (1 - cavity[elem]).astype(F32)


def operate(faces, shift, cavity, elems, packed, out, own_rows, begin, end):
    def product(left, right):
        return lax.dot_general(
            left, right, (((1,), (1,)), ((), ())), preferred_element_type=F32
        )

    def one(elem):
        at = [LAYER + elem]
        for side in range(SIDES - 1):
            beside = faces[side, elem]
            at.append(jnp.where(beside < 0, NONE, jnp.clip(beside + shift, 0, NONE - 1)))
        pieces = []
        for piece in range(3):
            pairs = [
                elems[0, at[2 * pair], piece] + elems[1, at[2 * pair + 1], piece]
                for pair in range(3)
            ]
            pairs.append(elems[0, at[6], piece])
            pieces.append(jnp.concatenate(pairs, axis=1))
        three = product(jnp.concatenate(pieces, axis=0), packed[elem, 0])
        two = product(jnp.concatenate(pieces[:2], axis=0), packed[elem, 1])
        last = product(pieces[0], packed[elem, 2])
        small = three[2 * NARROW :] + two[NARROW:] + last
        value = three[:NARROW] + (three[NARROW : 2 * NARROW] + two[:NARROW] + small)
        return value * solid(cavity, elem)

    def body(pair, carry):
        cols = pl.ds(pl.multiple_of(pair * 128, 128), 128)
        out[own_rows, cols] = jnp.concatenate([one(2 * pair), one(2 * pair + 1)], axis=1)
        return carry

    lax.fori_loop(begin, end, body, 0, unroll=4)


def kernel(
    faces,
    cavity,
    start,
    blocks,
    basis_out,
    coef_out,
    basis,
    image,
    second,
    send_0,
    low_0,
    high_0,
    send_1,
    low_1,
    high_1,
    elems,
    packed,
    staged,
    near_0,
    far_0,
    done_0,
    near_1,
    far_1,
    done_1,
    near_2,
    far_2,
    done_2,
    near_3,
    far_3,
    done_3,
    part_0,
    part_1,
    part_2,
    part_3,
    gram,
    upper,
    inverse,
    alpha,
    flip,
    stage_sem,
    halo_send,
    halo_recv,
    rows_send,
    rows_recv,
    sums_send,
    sums_recv,
):
    space = lax.axis_index("space")
    blk = lax.axis_index("blk")
    core = lax.rem(space, CORES)
    spot = lax.rem(space, XS * CORES)
    plane = space // (XS * CORES)
    plane_base = plane * (XS * CORES)
    quad = blk * CORES + core
    right = lax.rem(blk + 1, YS)
    left = lax.rem(blk + YS - 1, YS)
    shift = LAYER - space * LAYER
    own_rows = pl.ds(pl.multiple_of(blk * NARROW, NARROW), NARROW)
    right_rows = pl.ds(pl.multiple_of(right * NARROW, NARROW), NARROW)
    left_rows = pl.ds(pl.multiple_of(left * NARROW, NARROW), NARROW)
    above = (lax.rem(space + 1, SPACE), blk)
    below = (lax.rem(space + SPACE - 1, SPACE), blk)
    near_ids = [lax.rem(spot + step, 8) for step in range(1, 8)]
    near_devices = [(plane_base + near, blk) for near in near_ids]
    far_devices = [(lax.rem(plane + step, 8) * 8 + spot, blk) for step in range(1, 8)]
    quads = [lax.rem(quad + step, 8) for step in range(1, 8)]
    done_devices = [(space - core + lax.rem(q, CORES), q // CORES) for q in quads]

    def stage_copy(part):
        return pltpu.make_async_copy(
            blocks.at[pl.ds(part * STAGED, STAGED)], staged.at[part % 2], stage_sem.at[part % 2]
        )

    stage_copy(0).start()
    stage_copy(1).start()
    barrier = pltpu.get_barrier_semaphore()
    for device in near_devices + far_devices + done_devices + [above, below]:
        pl.semaphore_signal(barrier, inc=1, device_id=device, device_id_type=MESH)

    def masked(array, rows, send, part):
        is_low = lax.broadcasted_iota(jnp.int32, (NARROW, 2 * DOF), 1) < DOF
        count = LAYER // 2 // PARTS
        for step in range(count):
            pair = part * count + step
            cols = pl.ds(pl.multiple_of(pair * 128, 128), 128)
            weight = jnp.where(is_low, solid(cavity, 2 * pair), solid(cavity, 2 * pair + 1))
            send[:, cols] = array[rows, cols] * weight

    def halo_copies(call, part, send, low, high):
        cols = pl.ds(pl.multiple_of(part * PART, PART), PART)
        return [
            pltpu.make_async_remote_copy(
                src_ref=send.at[:, cols],
                dst_ref=target.at[:, cols],
                send_sem=halo_send.at[call, way, part],
                recv_sem=halo_recv.at[call, way, part],
                device_id=device,
                device_id_type=MESH,
            )
            for way, target, device in ((0, low, above), (1, high, below))
        ]

    def rows_copy(call, slot, array, rows, half, target):
        place = array.at[rows, pl.ds(half * HALF, HALF)]
        return pltpu.make_async_remote_copy(
            src_ref=place,
            dst_ref=place,
            send_sem=rows_send.at[call, slot],
            recv_sem=rows_recv.at[call, slot],
            device_id=(space, target),
            device_id_type=MESH,
        )

    def gather(call, array):
        copies = [
            rows_copy(call, 0, array, own_rows, 0, right),
            rows_copy(call, 1, array, own_rows, 1, left),
            rows_copy(call, 2, array, own_rows, 1, right),
            rows_copy(call, 3, array, own_rows, 0, left),
        ]
        for copy in copies:
            copy.start()
        return copies

    def relay(call, array, copies):
        copies[0].wait_recv()
        onward = rows_copy(call, 4, array, left_rows, 0, right)
        onward.start()
        copies[1].wait_recv()
        back = rows_copy(call, 5, array, right_rows, 1, left)
        back.start()
        return copies + [onward, back]

    def gathered(copies):
        copies[0].wait_send()
        copies[1].wait_send()
        for copy in copies[2:]:
            copy.wait()

    def wait(copies):
        for copy in copies:
            copy.wait()

    def exchange(call, stage, sources, slots, mine, devices):
        copies = []
        for step in range(7):
            copy = pltpu.make_async_remote_copy(
                src_ref=sources[step],
                dst_ref=slots.at[mine],
                send_sem=sums_send.at[call, stage, step],
                recv_sem=sums_recv.at[call, stage, step],
                device_id=devices[step],
                device_id_type=MESH,
            )
            copy.start()
            copies.append(copy)
        return copies

    def total(slots):
        value = slots[0]
        for slot in range(1, 8):
            value = value + slots[slot]
        return value

    def reduce_near(call, part, near):
        half = part.shape[0] // CORES
        sources = [
            part.at[pl.ds(pl.multiple_of(lax.rem(spot_id, CORES) * half, 8), half)]
            for spot_id in near_ids
        ]
        copies = exchange(call, 0, sources, near, spot, near_devices)
        near[spot] = part[pl.ds(pl.multiple_of(core * half, 8), half), :]
        return copies

    def reduce_far(call, copies, near, far):
        wait(copies)
        far[plane] = total(near)
        return exchange(call, 1, [far.at[plane]] * 7, far, plane, far_devices)

    def reduce_done(call, copies, far, done):
        wait(copies)
        done[quad] = total(far)
        return exchange(call, 2, [done.at[quad]] * 7, done, quad, done_devices)

    def square(done, which):
        rows = []
        for member in range(YS):
            panel = jnp.concatenate([done[2 * member], done[2 * member + 1]], axis=0)
            rows.append(panel[which * NARROW : (which + 1) * NARROW])
        return jnp.concatenate(rows, axis=0)

    def over_chunks(body, init):
        def step(chunk, carry):
            return body(pl.ds(pl.multiple_of(chunk * CHUNK, CHUNK), CHUNK), carry)

        return lax.fori_loop(0, ROWS // CHUNK, step, init)

    def over_parts(body):
        def step(part, carry):
            body(part)
            return carry

        lax.fori_loop(0, PARTS, step, 0)

    def keep_upper(which):
        flip[...] = upper[...].T
        coef_out[which] = flip[own_rows, :]

    def receive(call, send, low, high):
        def body(part):
            for copy in halo_copies(call, part, send, low, high):
                copy.wait()
            spread(low, elems, 0, part)
            spread(high, elems, 2 * LAYER, part)

        over_parts(body)

    def apply(out, begin, end):
        operate(faces, shift, cavity, elems, packed, out, own_rows, begin, end)

    basis[own_rows, :] = start[...]
    over_parts(lambda part: masked(start, slice(None), send_0, part))
    pl.semaphore_wait(barrier, 23)

    def start_halo(part):
        for copy in halo_copies(0, part, send_0, low_0, high_0):
            copy.start()

    over_parts(start_halo)
    start_copies = gather(0, basis)
    for part in range(LAYER // STAGED):
        stage_copy(part).wait()
        prepare(staged.at[part % 2], packed, part * STAGED)
        if part + 2 < LAYER // STAGED:
            stage_copy(part + 2).start()
    for which in range(2):
        for piece in range(3):
            elems[which, NONE, piece] = jnp.zeros((NARROW, 2 * DOF), BF16)
    over_parts(lambda part: spread(send_0, elems, LAYER, part))
    start_copies = relay(0, basis, start_copies)
    receive(0, send_0, low_0, high_0)
    apply(image, 0, LAYER // 2)
    image_copies = gather(1, image)
    gathered(start_copies)

    def start_products(cols, carry):
        own = jnp.concatenate([basis[own_rows, cols], image[own_rows, cols]], axis=0)
        return carry + cross(own, basis[:, cols])

    part_0[...] = over_chunks(start_products, jnp.zeros(part_0.shape, F32))
    sums = reduce_near(0, part_0, near_0)
    sums = reduce_far(0, sums, near_0, far_0)
    image_copies = relay(1, image, image_copies)
    wait(reduce_done(0, sums, far_0, done_0))
    gram[...] = square(done_0, 0)
    factor_gram(gram, upper, inverse)
    alpha[...] = cross(times(inverse[...], square(done_0, 1)), inverse[...])
    gathered(image_copies)

    def first_residue(part):
        for side in range(PART // CHUNK):
            cols = pl.ds(pl.multiple_of(part * PART + side * CHUNK, CHUNK), CHUNK)
            vectors = times(inverse[...], basis[:, cols])
            basis[:, cols] = vectors
            image[:, cols] = times(inverse[...], image[:, cols]) - times(alpha[...], vectors)
        masked(image, own_rows, send_1, part)
        for copy in halo_copies(1, part, send_1, low_1, high_1):
            copy.start()

    over_parts(first_residue)

    def residue_products(cols, carry):
        own = image[own_rows, cols]
        return carry[0] + cross(own, image[:, cols]), carry[1] + cross(own, basis[:, cols])

    empty = jnp.zeros((NARROW, K), F32)
    products = over_chunks(residue_products, (empty, empty))
    part_1[pl.ds(0, NARROW), :] = products[0]
    part_1[pl.ds(NARROW, NARROW), :] = products[1]
    sums = reduce_near(1, part_1, near_1)
    coef_out[1] = alpha[own_rows, :]
    keep_upper(0)
    over_parts(lambda part: spread(send_1, elems, LAYER, part))
    receive(1, send_1, low_1, high_1)
    sums = reduce_far(1, sums, near_1, far_1)
    apply(second, 0, LAYER // 2)
    second_copies = gather(2, second)
    sums = reduce_done(1, sums, far_1, done_1)

    def image_products(cols, carry):
        return carry + cross(second[own_rows, cols], image[:, cols])

    part_2[...] = over_chunks(image_products, empty)
    inner_sums = reduce_near(2, part_2, near_2)
    wait(sums)
    gram[...] = square(done_1, 0)
    for first in range(0, K, WIDE):
        factor_rows(gram, upper, inverse, first)
        if first == WIDE:
            inner_sums = reduce_far(2, inner_sums, near_2, far_2)
    second_copies = relay(2, second, second_copies)
    skew = cross(upper[...], times(inverse[...], square(done_1, 1)))
    inner_sums = reduce_done(2, inner_sums, far_2, done_2)

    def second_basis(cols, carry):
        image[:, cols] = times(inverse[...], image[:, cols])
        return carry

    over_chunks(second_basis, 0)
    gathered(second_copies)

    def second_image(cols, carry):
        value = times(inverse[...], second[:, cols])
        second[:, cols] = value - times(upper[...], basis[:, cols])
        return carry

    over_chunks(second_image, 0)
    keep_upper(2)
    wait(inner_sums)
    inner = cross(times(inverse[...], square(done_2, 0)), inverse[...])
    alpha[...] = inner - skew

    def second_residue(cols, carry):
        value = second[:, cols] - times(alpha[...], image[:, cols])
        second[:, cols] = value
        return carry + cross(second[own_rows, cols], value)

    part_3[...] = over_chunks(second_residue, empty)
    sums = reduce_near(3, part_3, near_3)
    coef_out[3] = alpha[own_rows, :]
    sums = reduce_far(3, sums, near_3, far_3)
    wait(reduce_done(3, sums, far_3, done_3))
    gram[...] = square(done_3, 0)
    factor_gram(gram, upper, inverse)
    keep_upper(4)

    def last_basis(cols, carry):
        basis_out[:, cols] = times(inverse[own_rows, :], second[:, cols])
        return carry

    over_chunks(last_basis, 0)


def local(start, faces, cavity, blocks):
    smem = pl.BlockSpec(memory_space=pltpu.SMEM)
    vmem = pl.BlockSpec(memory_space=pltpu.VMEM)

    def slots(rows):
        return [pltpu.VMEM((8, rows // CORES, K), F32)] * 3

    basis, coefficients = pl.pallas_call(
        kernel,
        out_shape=(
            jax.ShapeDtypeStruct((NARROW, ROWS), F32),
            jax.ShapeDtypeStruct((5, NARROW, K), F32),
        ),
        in_specs=[
            smem,
            smem,
            vmem,
            pl.BlockSpec(memory_space=pl.ANY),
        ],
        out_specs=(vmem, vmem),
        scratch_shapes=[pltpu.VMEM((K, ROWS), F32)] * 3
        + [pltpu.VMEM((NARROW, ROWS), F32)] * 6
        + [
            pltpu.VMEM((2, NONE + 1, 3, NARROW, 2 * DOF), BF16),
            pltpu.VMEM((LAYER, 3, DOF, 8 * DOF), BF16),
            pltpu.VMEM((2, STAGED, SIDES, DOF, DOF), F32),
        ]
        + slots(2 * NARROW)
        + slots(2 * NARROW)
        + slots(NARROW)
        + slots(NARROW)
        + [pltpu.VMEM((count * NARROW, K), F32) for count in (2, 2, 1, 1)]
        + [pltpu.VMEM((K, K), F32)] * 5
        + [
            pltpu.SemaphoreType.DMA((2,)),
            pltpu.SemaphoreType.DMA((2, 2, PARTS)),
            pltpu.SemaphoreType.DMA((2, 2, PARTS)),
            pltpu.SemaphoreType.DMA((3, 6)),
            pltpu.SemaphoreType.DMA((3, 6)),
            pltpu.SemaphoreType.DMA((4, 3, 7)),
            pltpu.SemaphoreType.DMA((4, 3, 7)),
        ],
        compiler_params=pltpu.CompilerParams(
            collective_id=1, has_side_effects=True, vmem_limit_bytes=60 * 2**20
        ),
    )(faces.T, cavity, start.T, blocks)
    return basis.T, jnp.swapaxes(coefficients, 1, 2)


def solution(mesh):
    in_specs = (P("space", "blk"), P("space", None), P("space"), P("space", None, None, None))
    out_specs = (P("space", "blk"), P(None, None, "blk"))
    return jax.shard_map(local, mesh=mesh, in_specs=in_specs, out_specs=out_specs, check_vma=False)
```

time: 158 us -> 139 us (0.88)
  Pallas kernels: 151 us -> 135 us
  local copies, waits for them, and re-layouts: 4.98 us -> 3.4 us
    pallas_call x1, Pallas kernels: 151 us -> 135 us  [local(): pl.pallas_call(kernel, out_shape=(jax.ShapeDtypeStruct((NARROW, ROWS), F3...]
where the time goes in v2:
time: 139 us
  Pallas kernels  135 us (97%)
  local copies, waits for them, and re-layouts  3.4 us (2%)
    pallas_call x1, Pallas kernels, local(): pl.pallas_call(kernel, out_shape=(jax.ShapeDtypeStruct((NARROW, ROWS), F3...  135 us
    unnamed x2, local copies, waits for them, and re-layouts  3.4 us

profile of v2, /device:TPU:1, one launch (start us, length us, event | category | flops | bytes accessed | tf_op | source)
XLA Modules:
  0.0 138.7 jit_solution(498095280510646427)
XLA Ops:
  0.6 134.7 %shard_map.59 = (f32[32,4096]{1,0:T(8,128)}, f32[5,32,128]{2,1,0:T(8,128)}) custom-call(s32[6,64]{1,0:T(8,128)} %bitcast.7, s32[64]{0:T(128)} %cavity.1, f32[32,4096]{1,0:T(8,128)} %bitcast.4, f32[64,7,64,64]{3,2,1,0:T(8,128)} %blocks.1), custom_call_target="tpu_custom_call" | custom-call | tf_op jit(solution)/shard_map/pallas_call | solution.py:525
  135.3 1.9 %copy.8 = f32[4096,32]{0,1:T(8,128)} copy(f32[4096,32]{0,1:T(8,128)} %bitcast.5) | data formatting | bytes 1048576
  137.2 1.5 %copy.9 = f32[5,128,32]{1,2,0:T(8,128)} copy(f32[5,128,32]{1,2,0:T(8,128)} %bitcast.6) | data formatting | bytes 163840

commit v3 on v2

--- a/solution.py
+++ b/solution.py
@@ -115,7 +115,6 @@
 
 def spread(source, elems, base, part):
     is_low = lax.broadcasted_iota(jnp.int32, (NARROW, 2 * DOF), 1) < DOF
-
     count = LAYER // 2 // PARTS
 
     def body(step, carry):
@@ -130,7 +129,7 @@
                 elems[1, place, piece] = value
         return carry
 
-    lax.fori_loop(0, count, body, 0, unroll=2)
+    lax.fori_loop(0, count, body, 0, unroll=8)
 
 
 def solid(cavity, elem):
@@ -211,6 +210,7 @@
     inverse,
     alpha,
     flip,
+    update,
     stage_sem,
     halo_send,
     halo_recv,
@@ -285,12 +285,10 @@
             device_id_type=MESH,
         )
 
-    def gather(call, array):
+    def gather(call, array, half):
         copies = [
-            rows_copy(call, 0, array, own_rows, 0, right),
-            rows_copy(call, 1, array, own_rows, 1, left),
-            rows_copy(call, 2, array, own_rows, 1, right),
-            rows_copy(call, 3, array, own_rows, 0, left),
+            rows_copy(call, 2 * half, array, own_rows, half, (right, left)[half]),
+            rows_copy(call, 2 * half + 1, array, own_rows, half, (left, right)[half]),
         ]
         for copy in copies:
             copy.start()
@@ -300,20 +298,24 @@
         copies[0].wait_recv()
         onward = rows_copy(call, 4, array, left_rows, 0, right)
         onward.start()
-        copies[1].wait_recv()
+        copies[2].wait_recv()
         back = rows_copy(call, 5, array, right_rows, 1, left)
         back.start()
         return copies + [onward, back]
 
     def gathered(copies):
-        copies[0].wait_send()
-        copies[1].wait_send()
-        for copy in copies[2:]:
-            copy.wait()
+        for slot, copy in enumerate(copies):
+            if slot not in (0, 2):
+                copy.wait_recv()
+        for copy in copies:
+            copy.wait_send()
+
+    sent = []
 
     def wait(copies):
         for copy in copies:
-            copy.wait()
+            copy.wait_recv()
+        sent.extend(copies)
 
     def exchange(call, stage, sources, slots, mine, devices):
         copies = []
@@ -380,14 +382,16 @@
         flip[...] = upper[...].T
         coef_out[which] = flip[own_rows, :]
 
-    def receive(call, send, low, high):
-        def body(part):
+    def receive(call, send, low, high, first, count):
+        def body(step, carry):
+            part = first + step
             for copy in halo_copies(call, part, send, low, high):
                 copy.wait()
             spread(low, elems, 0, part)
             spread(high, elems, 2 * LAYER, part)
-
-        over_parts(body)
+            return carry
+
+        lax.fori_loop(0, count, body, 0)
 
     def apply(out, begin, end):
         operate(faces, shift, cavity, elems, packed, out, own_rows, begin, end)
@@ -401,7 +405,7 @@
             copy.start()
 
     over_parts(start_halo)
-    start_copies = gather(0, basis)
+    start_copies = gather(0, basis, 0) + gather(0, basis, 1)
     for part in range(LAYER // STAGED):
         stage_copy(part).wait()
         prepare(staged.at[part % 2], packed, part * STAGED)
@@ -412,9 +416,11 @@
             elems[which, NONE, piece] = jnp.zeros((NARROW, 2 * DOF), BF16)
     over_parts(lambda part: spread(send_0, elems, LAYER, part))
     start_copies = relay(0, basis, start_copies)
-    receive(0, send_0, low_0, high_0)
-    apply(image, 0, LAYER // 2)
-    image_copies = gather(1, image)
+    receive(0, send_0, low_0, high_0, 0, PARTS)
+    apply(image, 0, LAYER // 4)
+    image_copies = gather(1, image, 0)
+    apply(image, LAYER // 4, LAYER // 2)
+    image_copies += gather(1, image, 1)
     gathered(start_copies)
 
     def start_products(cols, carry):
@@ -429,14 +435,15 @@
     gram[...] = square(done_0, 0)
     factor_gram(gram, upper, inverse)
     alpha[...] = cross(times(inverse[...], square(done_0, 1)), inverse[...])
+    update[:, pl.ds(0, K)] = inverse[...]
+    update[:, pl.ds(K, K)] = -times(alpha[...], inverse[...])
     gathered(image_copies)
 
     def first_residue(part):
         for side in range(PART // CHUNK):
             cols = pl.ds(pl.multiple_of(part * PART + side * CHUNK, CHUNK), CHUNK)
-            vectors = times(inverse[...], basis[:, cols])
-            basis[:, cols] = vectors
-            image[:, cols] = times(inverse[...], image[:, cols]) - times(alpha[...], vectors)
+            both = jnp.concatenate([image[:, cols], basis[:, cols]], axis=0)
+            image[:, cols] = times(update[...], both)
         masked(image, own_rows, send_1, part)
         for copy in halo_copies(1, part, send_1, low_1, high_1):
             copy.start()
@@ -445,7 +452,9 @@
 
     def residue_products(cols, carry):
         own = image[own_rows, cols]
-        return carry[0] + cross(own, image[:, cols]), carry[1] + cross(own, basis[:, cols])
+        vectors = times(inverse[...], basis[:, cols])
+        basis[:, cols] = vectors
+        return carry[0] + cross(own, image[:, cols]), carry[1] + cross(own, vectors)
 
     empty = jnp.zeros((NARROW, K), F32)
     products = over_chunks(residue_products, (empty, empty))
@@ -455,11 +464,14 @@
     coef_out[1] = alpha[own_rows, :]
     keep_upper(0)
     over_parts(lambda part: spread(send_1, elems, LAYER, part))
-    receive(1, send_1, low_1, high_1)
+    receive(1, send_1, low_1, high_1, 0, 3)
     sums = reduce_far(1, sums, near_1, far_1)
-    apply(second, 0, LAYER // 2)
-    second_copies = gather(2, second)
+    receive(1, send_1, low_1, high_1, 3, 1)
+    apply(second, 0, LAYER // 4)
+    second_copies = gather(2, second, 0)
     sums = reduce_done(1, sums, far_1, done_1)
+    apply(second, LAYER // 4, LAYER // 2)
+    second_copies += gather(2, second, 1)
 
     def image_products(cols, carry):
         return carry + cross(second[own_rows, cols], image[:, cols])
@@ -475,27 +487,24 @@
     second_copies = relay(2, second, second_copies)
     skew = cross(upper[...], times(inverse[...], square(done_1, 1)))
     inner_sums = reduce_done(2, inner_sums, far_2, done_2)
+    update[:, pl.ds(0, K)] = inverse[...]
 
     def second_basis(cols, carry):
         image[:, cols] = times(inverse[...], image[:, cols])
+        basis[:, cols] = times(upper[...], basis[:, cols])
         return carry
 
     over_chunks(second_basis, 0)
-    gathered(second_copies)
-
-    def second_image(cols, carry):
-        value = times(inverse[...], second[:, cols])
-        second[:, cols] = value - times(upper[...], basis[:, cols])
-        return carry
-
-    over_chunks(second_image, 0)
     keep_upper(2)
     wait(inner_sums)
     inner = cross(times(inverse[...], square(done_2, 0)), inverse[...])
     alpha[...] = inner - skew
+    update[:, pl.ds(K, K)] = -alpha[...]
+    gathered(second_copies)
 
     def second_residue(cols, carry):
-        value = second[:, cols] - times(alpha[...], image[:, cols])
+        both = jnp.concatenate([second[:, cols], image[:, cols]], axis=0)
+        value = times(update[...], both) - basis[:, cols]
         second[:, cols] = value
         return carry + cross(second[own_rows, cols], value)
 
@@ -513,6 +522,8 @@
         return carry
 
     over_chunks(last_basis, 0)
+    for copy in sent:
+        copy.wait_send()
 
 
 def local(start, faces, cavity, blocks):
@@ -548,6 +559,7 @@
         + slots(NARROW)
         + [pltpu.VMEM((count * NARROW, K), F32) for count in (2, 2, 1, 1)]
         + [pltpu.VMEM((K, K), F32)] * 5
+        + [pltpu.VMEM((K, 2 * K), F32)]
         + [
             pltpu.SemaphoreType.DMA((2,)),
             pltpu.SemaphoreType.DMA((2, 2, PARTS)),

time: 139 us -> 129 us (0.928)
  Pallas kernels: 135 us -> 125 us
    pallas_call x1, Pallas kernels: 135 us -> 125 us  [local(): pl.pallas_call(kernel, out_shape=(jax.ShapeDtypeStruct((NARROW, ROWS), F3...]
where the time goes in v3:
time: 129 us
  Pallas kernels  125 us (97%)
  local copies, waits for them, and re-layouts  3.4 us (3%)
    pallas_call x1, Pallas kernels, local(): pl.pallas_call(kernel, out_shape=(jax.ShapeDtypeStruct((NARROW, ROWS), F3...  125 us
    unnamed x2, local copies, waits for them, and re-layouts  3.4 us

profile of v3, /device:TPU:1, one launch (start us, length us, event | category | flops | bytes accessed | tf_op | source)
XLA Modules:
  0.0 128.9 jit_solution(5749392550276108163)
XLA Ops:
  0.6 124.9 %shard_map.59 = (f32[32,4096]{1,0:T(8,128)}, f32[5,32,128]{2,1,0:T(8,128)}) custom-call(s32[6,64]{1,0:T(8,128)} %bitcast.7, s32[64]{0:T(128)} %cavity.1, f32[32,4096]{1,0:T(8,128)} %bitcast.4, f32[64,7,64,64]{3,2,1,0:T(8,128)} %blocks.1), custom_call_target="tpu_custom_call" | custom-call | tf_op jit(solution)/shard_map/pallas_call | solution.py:536
  125.5 1.9 %copy.8 = f32[4096,32]{0,1:T(8,128)} copy(f32[4096,32]{0,1:T(8,128)} %bitcast.5) | data formatting | bytes 1048576
  127.4 1.5 %copy.9 = f32[5,128,32]{1,2,0:T(8,128)} copy(f32[5,128,32]{1,2,0:T(8,128)} %bitcast.6) | data formatting | bytes 163840

commit v4 on v3

--- a/solution.py
+++ b/solution.py
@@ -21,7 +21,7 @@
 HALF = ROWS // 2
 NONE = 3 * LAYER
 WIDE = 32
-SUB = 8
+SUB = 16
 CHUNK = 512
 STAGED = 16
 MESH = pl.DeviceIdType.MESH
@@ -211,6 +211,7 @@
     alpha,
     flip,
     update,
+    start_sem,
     stage_sem,
     halo_send,
     halo_recv,
@@ -245,6 +246,8 @@
             blocks.at[pl.ds(part * STAGED, STAGED)], staged.at[part % 2], stage_sem.at[part % 2]
         )
 
+    load_start = pltpu.make_async_copy(start, basis.at[own_rows], start_sem)
+    load_start.start()
     stage_copy(0).start()
     stage_copy(1).start()
     barrier = pltpu.get_barrier_semaphore()
@@ -396,8 +399,8 @@
     def apply(out, begin, end):
         operate(faces, shift, cavity, elems, packed, out, own_rows, begin, end)
 
-    basis[own_rows, :] = start[...]
-    over_parts(lambda part: masked(start, slice(None), send_0, part))
+    load_start.wait()
+    over_parts(lambda part: masked(basis, own_rows, send_0, part))
     pl.semaphore_wait(barrier, 23)
 
     def start_halo(part):
@@ -417,11 +420,9 @@
     over_parts(lambda part: spread(send_0, elems, LAYER, part))
     start_copies = relay(0, basis, start_copies)
     receive(0, send_0, low_0, high_0, 0, PARTS)
-    apply(image, 0, LAYER // 4)
-    image_copies = gather(1, image, 0)
-    apply(image, LAYER // 4, LAYER // 2)
-    image_copies += gather(1, image, 1)
+    apply(image, 0, LAYER // 2)
     gathered(start_copies)
+    image_copies = gather(1, image, 0) + gather(1, image, 1)
 
     def start_products(cols, carry):
         own = jnp.concatenate([basis[own_rows, cols], image[own_rows, cols]], axis=0)
@@ -430,8 +431,9 @@
     part_0[...] = over_chunks(start_products, jnp.zeros(part_0.shape, F32))
     sums = reduce_near(0, part_0, near_0)
     sums = reduce_far(0, sums, near_0, far_0)
+    sums = reduce_done(0, sums, far_0, done_0)
     image_copies = relay(1, image, image_copies)
-    wait(reduce_done(0, sums, far_0, done_0))
+    wait(sums)
     gram[...] = square(done_0, 0)
     factor_gram(gram, upper, inverse)
     alpha[...] = cross(times(inverse[...], square(done_0, 1)), inverse[...])
@@ -464,12 +466,12 @@
     coef_out[1] = alpha[own_rows, :]
     keep_upper(0)
     over_parts(lambda part: spread(send_1, elems, LAYER, part))
-    receive(1, send_1, low_1, high_1, 0, 3)
+    receive(1, send_1, low_1, high_1, 0, 2)
     sums = reduce_far(1, sums, near_1, far_1)
-    receive(1, send_1, low_1, high_1, 3, 1)
+    receive(1, send_1, low_1, high_1, 2, 2)
     apply(second, 0, LAYER // 4)
+    sums = reduce_done(1, sums, far_1, done_1)
     second_copies = gather(2, second, 0)
-    sums = reduce_done(1, sums, far_1, done_1)
     apply(second, LAYER // 4, LAYER // 2)
     second_copies += gather(2, second, 1)
 
@@ -480,13 +482,10 @@
     inner_sums = reduce_near(2, part_2, near_2)
     wait(sums)
     gram[...] = square(done_1, 0)
-    for first in range(0, K, WIDE):
-        factor_rows(gram, upper, inverse, first)
-        if first == WIDE:
-            inner_sums = reduce_far(2, inner_sums, near_2, far_2)
+    factor_gram(gram, upper, inverse)
+    skew = cross(upper[...], times(inverse[...], square(done_1, 1)))
+    inner_sums = reduce_far(2, inner_sums, near_2, far_2)
     second_copies = relay(2, second, second_copies)
-    skew = cross(upper[...], times(inverse[...], square(done_1, 1)))
-    inner_sums = reduce_done(2, inner_sums, far_2, done_2)
     update[:, pl.ds(0, K)] = inverse[...]
 
     def second_basis(cols, carry):
@@ -495,6 +494,7 @@
         return carry
 
     over_chunks(second_basis, 0)
+    inner_sums = reduce_done(2, inner_sums, far_2, done_2)
     keep_upper(2)
     wait(inner_sums)
     inner = cross(times(inverse[...], square(done_2, 0)), inverse[...])
@@ -542,7 +542,7 @@
         in_specs=[
             smem,
             smem,
-            vmem,
+            pl.BlockSpec(memory_space=pl.ANY),
             pl.BlockSpec(memory_space=pl.ANY),
         ],
         out_specs=(vmem, vmem),
@@ -561,6 +561,7 @@
         + [pltpu.VMEM((K, K), F32)] * 5
         + [pltpu.VMEM((K, 2 * K), F32)]
         + [
+            pltpu.SemaphoreType.DMA,
             pltpu.SemaphoreType.DMA((2,)),
             pltpu.SemaphoreType.DMA((2, 2, PARTS)),
             pltpu.SemaphoreType.DMA((2, 2, PARTS)),

time: 129 us -> 128 us (level)
  no operation moved by 1% of the time
where the time goes in v4:
time: 128 us
  Pallas kernels  124 us (97%)
  local copies, waits for them, and re-layouts  3.4 us (3%)
    pallas_call x1, Pallas kernels, local(): pl.pallas_call(kernel, out_shape=(jax.ShapeDtypeStruct((NARROW, ROWS), F3...  124 us
    unnamed x2, local copies, waits for them, and re-layouts  3.4 us

profile of v4, /device:TPU:1, one launch (start us, length us, event | category | flops | bytes accessed | tf_op | source)
XLA Modules:
  0.0 128.2 jit_solution(4097401049947910548)
XLA Ops:
  0.6 124.2 %shard_map.59 = (f32[32,4096]{1,0:T(8,128)}, f32[5,32,128]{2,1,0:T(8,128)}) custom-call(s32[6,64]{1,0:T(8,128)} %bitcast.7, s32[64]{0:T(128)} %cavity.1, f32[32,4096]{1,0:T(8,128)} %bitcast.4, f32[64,7,64,64]{3,2,1,0:T(8,128)} %blocks.1), custom_call_target="tpu_custom_call" | custom-call | tf_op jit(solution)/shard_map/pallas_call | solution.py:536
  124.8 1.9 %copy.8 = f32[4096,32]{0,1:T(8,128)} copy(f32[4096,32]{0,1:T(8,128)} %bitcast.5) | data formatting | bytes 1048576
  126.7 1.5 %copy.9 = f32[5,128,32]{1,2,0:T(8,128)} copy(f32[5,128,32]{1,2,0:T(8,128)} %bitcast.6) | data formatting | bytes 163840

commit v5 on v4

--- a/solution.py
+++ b/solution.py
@@ -277,10 +277,10 @@
             for way, target, device in ((0, low, above), (1, high, below))
         ]
 
-    def rows_copy(call, slot, array, rows, half, target):
+    def rows_copy(call, slot, array, rows, half, target, source=None):
         place = array.at[rows, pl.ds(half * HALF, HALF)]
         return pltpu.make_async_remote_copy(
-            src_ref=place,
+            src_ref=place if source is None else source.at[:, pl.ds(half * HALF, HALF)],
             dst_ref=place,
             send_sem=rows_send.at[call, slot],
             recv_sem=rows_recv.at[call, slot],
@@ -288,10 +288,10 @@
             device_id_type=MESH,
         )
 
-    def gather(call, array, half):
+    def gather(call, array, half, source=None):
         copies = [
-            rows_copy(call, 2 * half, array, own_rows, half, (right, left)[half]),
-            rows_copy(call, 2 * half + 1, array, own_rows, half, (left, right)[half]),
+            rows_copy(call, 2 * half, array, own_rows, half, (right, left)[half], source),
+            rows_copy(call, 2 * half + 1, array, own_rows, half, (left, right)[half], source),
         ]
         for copy in copies:
             copy.start()
@@ -402,13 +402,13 @@
     load_start.wait()
     over_parts(lambda part: masked(basis, own_rows, send_0, part))
     pl.semaphore_wait(barrier, 23)
+    start_copies = gather(0, basis, 0, start) + gather(0, basis, 1, start)
 
     def start_halo(part):
         for copy in halo_copies(0, part, send_0, low_0, high_0):
             copy.start()
 
     over_parts(start_halo)
-    start_copies = gather(0, basis, 0) + gather(0, basis, 1)
     for part in range(LAYER // STAGED):
         stage_copy(part).wait()
         prepare(staged.at[part % 2], packed, part * STAGED)
@@ -463,29 +463,29 @@
     part_1[pl.ds(0, NARROW), :] = products[0]
     part_1[pl.ds(NARROW, NARROW), :] = products[1]
     sums = reduce_near(1, part_1, near_1)
+    over_parts(lambda part: spread(send_1, elems, LAYER, part))
+    receive(1, send_1, low_1, high_1, 0, PARTS)
+    sums = reduce_far(1, sums, near_1, far_1)
+    apply(second, 0, LAYER // 4)
+    second_copies = gather(2, second, 0)
+    apply(second, LAYER // 4, LAYER // 2)
+    sums = reduce_done(1, sums, far_1, done_1)
+    second_copies += gather(2, second, 1)
+
+    def image_products(cols, carry):
+        return carry + cross(second[own_rows, cols], image[:, cols])
+
+    part_2[...] = over_chunks(image_products, empty)
+    inner_sums = reduce_near(2, part_2, near_2)
     coef_out[1] = alpha[own_rows, :]
     keep_upper(0)
-    over_parts(lambda part: spread(send_1, elems, LAYER, part))
-    receive(1, send_1, low_1, high_1, 0, 2)
-    sums = reduce_far(1, sums, near_1, far_1)
-    receive(1, send_1, low_1, high_1, 2, 2)
-    apply(second, 0, LAYER // 4)
-    sums = reduce_done(1, sums, far_1, done_1)
-    second_copies = gather(2, second, 0)
-    apply(second, LAYER // 4, LAYER // 2)
-    second_copies += gather(2, second, 1)
-
-    def image_products(cols, carry):
-        return carry + cross(second[own_rows, cols], image[:, cols])
-
-    part_2[...] = over_chunks(image_products, empty)
-    inner_sums = reduce_near(2, part_2, near_2)
     wait(sums)
     gram[...] = square(done_1, 0)
+    inner_sums = reduce_far(2, inner_sums, near_2, far_2)
+    second_copies = relay(2, second, second_copies)
     factor_gram(gram, upper, inverse)
     skew = cross(upper[...], times(inverse[...], square(done_1, 1)))
-    inner_sums = reduce_far(2, inner_sums, near_2, far_2)
-    second_copies = relay(2, second, second_copies)
+    inner_sums = reduce_done(2, inner_sums, far_2, done_2)
     update[:, pl.ds(0, K)] = inverse[...]
 
     def second_basis(cols, carry):
@@ -494,7 +494,6 @@
         return carry
 
     over_chunks(second_basis, 0)
-    inner_sums = reduce_done(2, inner_sums, far_2, done_2)
     keep_upper(2)
     wait(inner_sums)
     inner = cross(times(inverse[...], square(done_2, 0)), inverse[...])

time: 128 us -> 126 us (0.984)
  Pallas kernels: 124 us -> 122 us
    pallas_call x1, Pallas kernels: 124 us -> 122 us  [local(): pl.pallas_call(kernel, out_shape=(jax.ShapeDtypeStruct((NARROW, ROWS), F3...]
where the time goes in v5:
time: 126 us
  Pallas kernels  122 us (97%)
  local copies, waits for them, and re-layouts  3.4 us (3%)
    pallas_call x1, Pallas kernels, local(): pl.pallas_call(kernel, out_shape=(jax.ShapeDtypeStruct((NARROW, ROWS), F3...  122 us
    unnamed x2, local copies, waits for them, and re-layouts  3.4 us

profile of v5, /device:TPU:1, one launch (start us, length us, event | category | flops | bytes accessed | tf_op | source)
XLA Modules:
  0.0 125.7 jit_solution(3147359038240047355)
XLA Ops:
  0.6 121.7 %shard_map.59 = (f32[32,4096]{1,0:T(8,128)}, f32[5,32,128]{2,1,0:T(8,128)}) custom-call(s32[6,64]{1,0:T(8,128)} %bitcast.7, s32[64]{0:T(128)} %cavity.1, f32[32,4096]{1,0:T(8,128)} %bitcast.4, f32[64,7,64,64]{3,2,1,0:T(8,128)} %blocks.1), custom_call_target="tpu_custom_call" | custom-call | tf_op jit(solution)/shard_map/pallas_call | solution.py:535
  122.3 1.9 %copy.8 = f32[4096,32]{0,1:T(8,128)} copy(f32[4096,32]{0,1:T(8,128)} %bitcast.5) | data formatting | bytes 1048576
  124.2 1.5 %copy.9 = f32[5,128,32]{1,2,0:T(8,128)} copy(f32[5,128,32]{1,2,0:T(8,128)} %bitcast.6) | data formatting | bytes 163840

commit v6 on v5

--- a/solution.py
+++ b/solution.py
@@ -20,6 +20,7 @@
 PART = ROWS // PARTS
 HALF = ROWS // 2
 NONE = 3 * LAYER
+STEPS = (4, 3, 5, 2, 6, 1, 7)
 WIDE = 32
 SUB = 16
 CHUNK = 512
@@ -235,10 +236,10 @@
     left_rows = pl.ds(pl.multiple_of(left * NARROW, NARROW), NARROW)
     above = (lax.rem(space + 1, SPACE), blk)
     below = (lax.rem(space + SPACE - 1, SPACE), blk)
-    near_ids = [lax.rem(spot + step, 8) for step in range(1, 8)]
+    near_ids = [lax.rem(spot + step, 8) for step in STEPS]
     near_devices = [(plane_base + near, blk) for near in near_ids]
-    far_devices = [(lax.rem(plane + step, 8) * 8 + spot, blk) for step in range(1, 8)]
-    quads = [lax.rem(quad + step, 8) for step in range(1, 8)]
+    far_devices = [(lax.rem(plane + step, 8) * 8 + spot, blk) for step in STEPS]
+    quads = [lax.rem(quad + step, 8) for step in STEPS]
     done_devices = [(space - core + lax.rem(q, CORES), q // CORES) for q in quads]
 
     def stage_copy(part):

time: 126 us -> 124 us (0.984)
  Pallas kernels: 122 us -> 120 us
    pallas_call x1, Pallas kernels: 122 us -> 120 us  [local(): pl.pallas_call(kernel, out_shape=(jax.ShapeDtypeStruct((NARROW, ROWS), F3...]
where the time goes in v6:
time: 124 us
  Pallas kernels  120 us (97%)
  local copies, waits for them, and re-layouts  3.4 us (3%)
    pallas_call x1, Pallas kernels, local(): pl.pallas_call(kernel, out_shape=(jax.ShapeDtypeStruct((NARROW, ROWS), F3...  120 us
    unnamed x2, local copies, waits for them, and re-layouts  3.4 us

profile of v6, /device:TPU:1, one launch (start us, length us, event | category | flops | bytes accessed | tf_op | source)
XLA Modules:
  0.0 123.9 jit_solution(5944478452207886536)
XLA Ops:
  0.6 119.9 %shard_map.59 = (f32[32,4096]{1,0:T(8,128)}, f32[5,32,128]{2,1,0:T(8,128)}) custom-call(s32[6,64]{1,0:T(8,128)} %bitcast.7, s32[64]{0:T(128)} %cavity.1, f32[32,4096]{1,0:T(8,128)} %bitcast.4, f32[64,7,64,64]{3,2,1,0:T(8,128)} %blocks.1), custom_call_target="tpu_custom_call" | custom-call | tf_op jit(solution)/shard_map/pallas_call | solution.py:536
  120.5 1.9 %copy.8 = f32[4096,32]{0,1:T(8,128)} copy(f32[4096,32]{0,1:T(8,128)} %bitcast.5) | data formatting | bytes 1048576
  122.4 1.5 %copy.9 = f32[5,128,32]{1,2,0:T(8,128)} copy(f32[5,128,32]{1,2,0:T(8,128)} %bitcast.6) | data formatting | bytes 163840

commit v7 on v6

--- a/solution.py
+++ b/solution.py
@@ -176,7 +176,8 @@
     cavity,
     start,
     blocks,
-    basis_out,
+    residue_out,
+    gram_out,
     coef_out,
     basis,
     image,
@@ -212,6 +213,7 @@
     alpha,
     flip,
     update,
+    residue_sem,
     start_sem,
     stage_sem,
     halo_send,
@@ -510,20 +512,33 @@
 
     part_3[...] = over_chunks(second_residue, empty)
     sums = reduce_near(3, part_3, near_3)
+    store_residue = pltpu.make_async_copy(second, residue_out, residue_sem)
+    store_residue.start()
     coef_out[3] = alpha[own_rows, :]
     sums = reduce_far(3, sums, near_3, far_3)
     wait(reduce_done(3, sums, far_3, done_3))
-    gram[...] = square(done_3, 0)
-    factor_gram(gram, upper, inverse)
-    keep_upper(4)
-
-    def last_basis(cols, carry):
-        basis_out[:, cols] = times(inverse[own_rows, :], second[:, cols])
-        return carry
-
-    over_chunks(last_basis, 0)
+    gram_out[...] = square(done_3, 0)
+    store_residue.wait()
     for copy in sent:
         copy.wait_send()
+
+
+def finish_kernel(residue, gram, coef, basis_out, coef_out, vectors, upper, inverse, flip, sem):
+    own_rows = pl.ds(pl.multiple_of(lax.axis_index("blk") * NARROW, NARROW), NARROW)
+    load = pltpu.make_async_copy(residue, vectors, sem)
+    load.start()
+    coef_out[pl.ds(0, 4)] = coef[...]
+    factor_gram(gram, upper, inverse)
+    flip[...] = upper[...].T
+    coef_out[4] = flip[own_rows, :]
+    load.wait()
+
+    def last_basis(chunk, carry):
+        cols = pl.ds(pl.multiple_of(chunk * CHUNK, CHUNK), CHUNK)
+        basis_out[:, cols] = times(inverse[own_rows, :], vectors[:, cols])
+        return carry
+
+    lax.fori_loop(0, ROWS // CHUNK, last_basis, 0)
 
 
 def local(start, faces, cavity, blocks):
@@ -533,11 +548,12 @@
     def slots(rows):
         return [pltpu.VMEM((8, rows // CORES, K), F32)] * 3
 
-    basis, coefficients = pl.pallas_call(
+    residue, gram, coefficients = pl.pallas_call(
         kernel,
         out_shape=(
-            jax.ShapeDtypeStruct((NARROW, ROWS), F32),
-            jax.ShapeDtypeStruct((5, NARROW, K), F32),
+            jax.ShapeDtypeStruct((K, ROWS), F32),
+            jax.ShapeDtypeStruct((K, K), F32),
+            jax.ShapeDtypeStruct((4, NARROW, K), F32),
         ),
         in_specs=[
             smem,
@@ -545,7 +561,7 @@
             pl.BlockSpec(memory_space=pl.ANY),
             pl.BlockSpec(memory_space=pl.ANY),
         ],
-        out_specs=(vmem, vmem),
+        out_specs=(pl.BlockSpec(memory_space=pl.ANY), vmem, vmem),
         scratch_shapes=[pltpu.VMEM((K, ROWS), F32)] * 3
         + [pltpu.VMEM((NARROW, ROWS), F32)] * 6
         + [
@@ -562,6 +578,7 @@
         + [pltpu.VMEM((K, 2 * K), F32)]
         + [
             pltpu.SemaphoreType.DMA,
+            pltpu.SemaphoreType.DMA,
             pltpu.SemaphoreType.DMA((2,)),
             pltpu.SemaphoreType.DMA((2, 2, PARTS)),
             pltpu.SemaphoreType.DMA((2, 2, PARTS)),
@@ -574,6 +591,19 @@
             collective_id=1, has_side_effects=True, vmem_limit_bytes=60 * 2**20
         ),
     )(faces.T, cavity, start.T, blocks)
+    basis, coefficients = pl.pallas_call(
+        finish_kernel,
+        out_shape=(
+            jax.ShapeDtypeStruct((NARROW, ROWS), F32),
+            jax.ShapeDtypeStruct((5, NARROW, K), F32),
+        ),
+        in_specs=[pl.BlockSpec(memory_space=pl.ANY), vmem, vmem],
+        out_specs=(vmem, vmem),
+        scratch_shapes=[pltpu.VMEM((K, ROWS), F32)]
+        + [pltpu.VMEM((K, K), F32)] * 3
+        + [pltpu.SemaphoreType.DMA],
+        compiler_params=pltpu.CompilerParams(vmem_limit_bytes=63 * 2**20),
+    )(residue, gram, coefficients)
     return basis.T, jnp.swapaxes(coefficients, 1, 2)
 
 

time: 124 us -> 124 us (level)
  local copies, waits for them, and re-layouts: 3.4 us -> 0 us
  Pallas kernels: 120 us -> 122 us
    unnamed x2 -> x0, local copies, waits for them, and re-layouts: 3.4 us -> none
    pallas_call x1 -> x2, Pallas kernels: 120 us -> 122 us  [the longest x1 114 us: local(): pl.pallas_call(kernel, out_shape=(jax.ShapeDtypeStruct((K, ROWS), F32), j...]
where the time goes in v7:
time: 124 us; the launch traced here: 123 us
  Pallas kernels  122 us (98%)
    pallas_call x1, Pallas kernels, local(): pl.pallas_call(kernel, out_shape=(jax.ShapeDtypeStruct((K, ROWS), F32), j...  114 us
    pallas_call x1, Pallas kernels, local(): pl.pallas_call(finish_kernel, out_shape=(jax.ShapeDtypeStruct((NARROW, RO...  8.17 us

profile of v7, /device:TPU:1, one launch (start us, length us, event | category | flops | bytes accessed | tf_op | source)
XLA Modules:
  0.0 123.3 jit_solution(9968160826308754711)
XLA Ops:
  0.6 114.3 %shard_map.59 = (f32[128,4096]{1,0:T(8,128)}, f32[128,128]{1,0:T(8,128)}, f32[4,32,128]{2,1,0:T(8,128)}) custom-call(s32[6,64]{1,0:T(8,128)} %bitcast.5, s32[64]{0:T(128)} %cavity.1, f32[32,4096]{1,0:T(8,128)} %bitcast.4, f32[64,7,64,64]{3,2,1,0:T(8,128)} %blocks.1), custom_call_target="tpu_custom_call" | custom-call | tf_op jit(solution)/shard_map/pallas_call | solution.py:551
  115.0 8.2 %shard_map.60 = (f32[32,4096]{1,0:T(8,128)}, f32[5,32,128]{2,1,0:T(8,128)}) custom-call(f32[128,4096]{1,0:T(8,128)} %get-tuple-element.7.residue, f32[128,128]{1,0:T(8,128)} %get-tuple-element.8.gram, f32[4,32,128]{2,1,0:T(8,128)} %get-tuple-element.9.coef), custom_call_target="tpu_custom_call" | custom-call | tf_op jit(solution)/shard_map/pallas_call | solution.py:594

commit v8 on v7

--- a/solution.py
+++ b/solution.py
@@ -23,7 +23,7 @@
 STEPS = (4, 3, 5, 2, 6, 1, 7)
 WIDE = 32
 SUB = 16
-CHUNK = 512
+CHUNK = 1024
 STAGED = 16
 MESH = pl.DeviceIdType.MESH
 F32 = jnp.float32

time: 124 us -> 120 us (0.968)
  Pallas kernels: 122 us -> 119 us
    pallas_call x1, Pallas kernels: 114 us -> 111 us  [local(): pl.pallas_call(kernel, out_shape=(jax.ShapeDtypeStruct((K, ROWS), F32), j...]
where the time goes in v8:
time: 120 us
  Pallas kernels  119 us (99%)
    pallas_call x1, Pallas kernels, local(): pl.pallas_call(kernel, out_shape=(jax.ShapeDtypeStruct((K, ROWS), F32), j...  111 us
    pallas_call x1, Pallas kernels, local(): pl.pallas_call(finish_kernel, out_shape=(jax.ShapeDtypeStruct((NARROW, RO...  7.56 us

profile of v8, /device:TPU:1, one launch (start us, length us, event | category | flops | bytes accessed | tf_op | source)
XLA Modules:
  0.0 119.5 jit_solution(5965623364646950849)
XLA Ops:
  0.6 111.2 %shard_map.59 = (f32[128,4096]{1,0:T(8,128)}, f32[128,128]{1,0:T(8,128)}, f32[4,32,128]{2,1,0:T(8,128)}) custom-call(s32[6,64]{1,0:T(8,128)} %bitcast.5, s32[64]{0:T(128)} %cavity.1, f32[32,4096]{1,0:T(8,128)} %bitcast.4, f32[64,7,64,64]{3,2,1,0:T(8,128)} %blocks.1), custom_call_target="tpu_custom_call" | custom-call | tf_op jit(solution)/shard_map/pallas_call | solution.py:551
  111.8 7.6 %shard_map.60 = (f32[32,4096]{1,0:T(8,128)}, f32[5,32,128]{2,1,0:T(8,128)}) custom-call(f32[128,4096]{1,0:T(8,128)} %get-tuple-element.7.residue, f32[128,128]{1,0:T(8,128)} %get-tuple-element.8.gram, f32[4,32,128]{2,1,0:T(8,128)} %get-tuple-element.9.coef), custom_call_target="tpu_custom_call" | custom-call | tf_op jit(solution)/shard_map/pallas_call | solution.py:594
